TPU v7x, 128 devices: a whole 4x4x4 slice. The times are simulated.
128 devices in a mesh: expert: 8 (over z_lo, y), dp: 16 (over z_hi, x, core).
Axes of the slice: x: 4, y: 4, z: 4 (z_hi: 2, z_lo: 2; z = z_hi * 2 + z_lo), core: 2. Of those that a mesh axis runs over, the one named last changes fastest.
Arguments:
- tokens: bfloat16 [2048, 7168], P('dp', 'expert'), may hold values from -6 to 6
- grad_out: bfloat16 [2048, 7168], P('dp', 'expert'), may hold values from -6 to 6
- expert_ids: int32 [2048, 2], P('dp'), may hold values from -1 to 7, as said below
- route_weights: float32 [2048, 2], P('dp'), may hold values from 0.1 to 1
- w_gate: bfloat16 [8, 7168, 2048], P('expert', 'dp'), may hold values from -0.0625 to 0.0625
- w_up: bfloat16 [8, 7168, 2048], P('expert', 'dp'), may hold values from -0.0625 to 0.0625
- w_down: bfloat16 [8, 2048, 7168], P('expert', None, 'dp'), may hold values from -0.125 to 0.125
Outputs:
- grad_tokens: bfloat16 [2048, 7168], P('dp', 'expert')
- grad_gate: bfloat16 [8, 7168, 2048], P('expert', 'dp')
- grad_up: bfloat16 [8, 7168, 2048], P('expert', 'dp')
- grad_down: bfloat16 [8, 2048, 7168], P('expert', None, 'dp')
Inputs may be any that keep to these rules, and one draw needn't show every extreme that they name: expert_ids[t, 0] is an expert; expert_ids[t, 1] is another expert or -1. Within each block of 128 rows (the tokens of one index of dp) no expert appears in more than 64 rows, and one expert, the same in every block, appears in exactly 64 rows, each of which has -1 as its second entry.
All inputs are finite; a program needn't handle non-finite values.
Results may differ from a plain program's by a relative error of at most 0.03.
Values may be sent and summed in bfloat16 or wider, within the bound.
A program may use at most 128 MiB of HBM per device.

v0:
```python
import math
import jax
import jax.numpy as jnp
from jax import lax
from jax.sharding import PartitionSpec as P


def body(tokens, grad_out, expert_ids, route_weights, w_gate, w_up, w_down):
    experts = lax.axis_size("expert")
    groups = lax.axis_size("dp")
    tok_rows = tokens.shape[0]
    capacity = tok_rows // 2
    hidden = w_gate.shape[2]
    slots = groups * capacity
    expert_index = lax.axis_index("expert")
    inv_root = 1.0 / math.sqrt(tok_rows * groups)
    rows_first = (((0,), (0,)), ((), ()))
    last_dims = (((1,), (1,)), ((), ()))
    routed = expert_ids >= 0
    matches = (
        expert_ids[:, :, None] == jnp.arange(experts, dtype=jnp.int32)[None, None, :]
    ).astype(jnp.int32)
    flat_match = matches.reshape(tok_rows * 2, experts)
    position = jnp.sum(flat_match * (jnp.cumsum(flat_match, axis=0) - 1), axis=1).reshape(
        tok_rows, 2
    )
    slot_ids = jnp.where(routed, expert_ids * capacity + position, -1)
    slot_match = (
        slot_ids[None, :, :] == jnp.arange(experts * capacity, dtype=jnp.int32)[:, None, None]
    ).astype(jnp.float32)
    dispatch = jnp.sum(slot_match, axis=2).astype(jnp.bfloat16)
    slot_weight = jnp.einsum("stk,tk->s", slot_match, route_weights)
    own_weight = lax.dynamic_slice_in_dim(slot_weight, expert_index * capacity, capacity)
    send_x = (
        jnp.dot(dispatch, tokens, preferred_element_type=jnp.float32)
        .astype(jnp.bfloat16)
        .reshape(experts, capacity, -1)
    )
    send_g = (
        jnp.dot(dispatch, grad_out, preferred_element_type=jnp.float32)
        .astype(jnp.bfloat16)
        .reshape(experts, capacity, -1)
    )
    recv_x, recv_g = (
        lax.all_to_all(
            lax.all_to_all(send_x, "expert", split_axis=0, concat_axis=2, tiled=True),
            "dp",
            split_axis=2,
            concat_axis=1,
            tiled=True,
        ),
        lax.all_to_all(
            lax.all_to_all(send_g, "expert", split_axis=0, concat_axis=2, tiled=True),
            "dp",
            split_axis=2,
            concat_axis=1,
            tiled=True,
        ),
    )
    feature_rows = recv_x.reshape(slots, -1)
    grad_rows = recv_g.reshape(slots, -1)
    gate_shard = w_gate[0]
    up_shard = w_up[0]
    down_shard = w_down[0]
    shard_width = gate_shard.shape[0]
    x_block = feature_rows
    g_block = grad_rows
    gate = jnp.dot(x_block, gate_shard, preferred_element_type=jnp.float32)
    upper = jnp.dot(x_block, up_shard, preferred_element_type=jnp.float32)
    back = lax.dot_general(g_block, down_shard, last_dims, preferred_element_type=jnp.float32)
    mine = lax.psum_scatter(
        jnp.concatenate([gate, upper, back], axis=1).astype(jnp.bfloat16),
        "dp",
        scatter_dimension=0,
        tiled=True,
    ).astype(jnp.float32)
    gate = mine[:, :hidden]
    upper = mine[:, hidden : 2 * hidden]
    back = mine[:, 2 * hidden :] * own_weight[:, None]
    sigmoid_gate = jax.nn.sigmoid(gate)
    scaled = own_weight[:, None] * gate * sigmoid_gate * upper
    d_gate = back * upper * sigmoid_gate * (1.0 + gate * (1.0 - sigmoid_gate))
    d_up = back * gate * sigmoid_gate
    local = jnp.concatenate([scaled, d_gate, d_up], axis=1).astype(jnp.bfloat16)
    piece = lax.all_gather(local, "dp", axis=0, tiled=True)
    x_block = feature_rows
    g_block = grad_rows
    scaled = piece[:, :hidden]
    d_gate = piece[:, hidden : 2 * hidden]
    d_up = piece[:, 2 * hidden :]
    grad_g = lax.dot_general(x_block, d_gate, rows_first, preferred_element_type=jnp.float32)
    grad_u = lax.dot_general(x_block, d_up, rows_first, preferred_element_type=jnp.float32)
    grad_d = lax.dot_general(scaled, g_block, rows_first, preferred_element_type=jnp.float32)
    block_dx = lax.dot_general(
        d_gate, gate_shard, last_dims, preferred_element_type=jnp.float32
    ) + lax.dot_general(d_up, up_shard, last_dims, preferred_element_type=jnp.float32)
    dx_rows = block_dx.astype(jnp.bfloat16)
    grad_g, grad_u, grad_d, dx_rows = (grad_g, grad_u, grad_d, dx_rows)
    returned = lax.all_to_all(
        lax.all_to_all(
            dx_rows.reshape(1, slots, shard_width), "dp", split_axis=1, concat_axis=2, tiled=True
        ),
        "expert",
        split_axis=2,
        concat_axis=0,
        tiled=True,
    )
    returned = returned.reshape(experts * capacity, -1)
    grad_tokens = lax.dot_general(
        dispatch, returned, rows_first, preferred_element_type=jnp.float32
    ).astype(jnp.bfloat16)
    grad_gate = (grad_g * inv_root).astype(jnp.bfloat16)[None]
    grad_up = (grad_u * inv_root).astype(jnp.bfloat16)[None]
    grad_down = (grad_d * inv_root).astype(jnp.bfloat16)[None]
    return (grad_tokens, grad_gate, grad_up, grad_down)


def solution(mesh):
    in_specs = (
        P("dp", "expert"),
        P("dp", "expert"),
        P("dp", None),
        P("dp", None),
        P("expert", "dp", None),
        P("expert", "dp", None),
        P("expert", None, "dp"),
    )
    out_specs = (
        P("dp", "expert"),
        P("expert", "dp", None),
        P("expert", "dp", None),
        P("expert", None, "dp"),
    )
    return jax.shard_map(body, mesh=mesh, in_specs=in_specs, out_specs=out_specs, check_vma=False)
```

profile of v0, /device:TPU:1, one launch (start us, length us, event | category | flops | bytes accessed | tf_op | source)
XLA Modules:
  0.0 595.4 jit_solution(15682744833489243268)
XLA Ops:
  7.2 0.9 copy.79
  8.4 0.6 reduce-window.6
  9.0 0.2 slice_reduce_fusion
  9.6 0.7 compare_select_fusion
  10.3 2.3 convolution_convert_fusion.3
  12.6 6.4 %all-to-all-start.2 = ((bf16[8,64,896]{2,1,0:T(8,128)(2,1)}), bf16[8,64,896]{2,1,0:T(8,128)(2,1)S(1)}, u32[]{:S(2)}, u32[]{:S(2)}) async-start(bf16[8,64,896]{2,1,0:T(8,128)(2,1)} %bitcast.12), calls=%async_computation.2 | async-start | bytes 1835008 | tf_op jit(solution)/shard_map/all_to_all | solution.py:53
  19.0 1.3 convolution_convert_fusion.4
  20.3 13.1 %all-to-all-done.2 = bf16[8,64,896]{2,1,0:T(8,128)(2,1)S(1)} async-done(((bf16[8,64,896]{2,1,0:T(8,128)(2,1)}), bf16[8,64,896]{2,1,0:T(8,128)(2,1)S(1)}, u32[]{:S(2)}, u32[]{:S(2)}) %all-to-all-start.2) | async-done | bytes 917536 | tf_op jit(solution)/shard_map/all_to_all | solution.py:53
  33.4 0.9 copy-done.1
  34.3 3.6 all-to-all-start
  37.9 2.6 copy.97
  40.4 11.1 %reshape.65 = bf16[1,64,7168]{1,0,2:T(2,128)(2,1)} reshape(bf16[1,64,8,896]{1,3,2,0:T(8,128)(2,1)} %copy.97) | data formatting | bytes 1835008 | tf_op jit(solution)/shard_map/all_to_all | solution.py:53
  51.6 0.5 broadcast.46
  52.1 41.0 %reduce.2 = bf16[7168,64]{1,0:T(8,128)(2,1)} reduce(bf16[7168,1,64]{2,1,0:T(2,128)(2,1)} %bitcast.92, bf16[]{:T(256)} %broadcast.46), dimensions={1}, to_apply=%bitcast.70.reduce_sub_computation | reduce | bytes 1835010
  93.1 4.3 reshape.68
  97.3 8.5 %all-to-all-start.3 = ((bf16[16,2,14336]{2,1,0:T(2,128)(2,1)}), bf16[16,2,14336]{2,1,0:T(2,128)(2,1)}, u32[]{:S(2)}, u32[]{:S(2)}) async-start(bf16[16,2,14336]{2,1,0:T(2,128)(2,1)} %reshape.68), calls=%async_computation.3 | async-start | bytes 1835008 | tf_op jit(solution)/shard_map/all_to_all | solution.py:52
  105.9 1.7 copy.96
  107.5 11.1 %reshape.64 = bf16[1,64,7168]{1,0,2:T(2,128)(2,1)} reshape(bf16[1,64,8,896]{1,3,2,0:T(8,128)(2,1)} %copy.96) | data formatting | bytes 1835008 | tf_op jit(solution)/shard_map/all_to_all | solution.py:46
  118.7 41.0 %reduce.3 = bf16[7168,64]{1,0:T(8,128)(2,1)} reduce(bf16[7168,1,64]{2,1,0:T(2,128)(2,1)} %bitcast.94, bf16[]{:T(256)} %broadcast.46), dimensions={1}, to_apply=%bitcast.72.reduce_sub_computation | reduce | bytes 1835010
  159.7 4.3 reshape.70
  163.9 7.2 %all-to-all-start.1 = ((bf16[16,2,14336]{2,1,0:T(2,128)(2,1)}), bf16[16,2,14336]{2,1,0:T(2,128)(2,1)}, u32[]{:S(2)}, u32[]{:S(2)}) async-start(bf16[16,2,14336]{2,1,0:T(2,128)(2,1)} %reshape.70), calls=%async_computation.1 | async-start | bytes 1835008 | tf_op jit(solution)/shard_map/all_to_all | solution.py:45
  171.2 0.4 reduce-scatter.2.cloned.1.call-start
  171.6 9.9 %reshape.69 = bf16[7168,1,64]{2,1,0:T(2,128)(2,1)} reshape(bf16[16,2,14336]{2,1,0:T(2,128)(2,1)} %all-to-all-done.3) | data formatting | bytes 1835008
  181.5 8.1 %copy.88 = bf16[1,64,7168]{2,1,0:T(8,128)(2,1)} copy(bf16[1,64,7168]{1,0,2:T(2,128)(2,1)} %bitcast.95) | data formatting | bytes 1835008 | tf_op jit(solution)/shard_map/all_to_all | solution.py:52
  189.7 2.3 all_to_all.84
  192.0 1.6 copy.89
  193.6 9.9 %reshape.71 = bf16[7168,1,64]{2,1,0:T(2,128)(2,1)} reshape(bf16[16,2,14336]{2,1,0:T(2,128)(2,1)} %all-to-all-done.1) | data formatting | bytes 1835008
  203.5 8.1 %copy.84 = bf16[1,64,7168]{2,1,0:T(8,128)(2,1)} copy(bf16[1,64,7168]{1,0,2:T(2,128)(2,1)} %bitcast.96) | data formatting | bytes 1835008 | tf_op jit(solution)/shard_map/all_to_all | solution.py:45
  211.7 2.3 all_to_all.77
  214.0 0.6 copy.85
  214.6 2.3 convolution_convert_fusion.1
  217.0 2.3 convolution_convert_fusion.2
  219.4 2.3 convolution_convert_fusion
  221.7 11.3 %pad_maximum_fusion = bf16[1024,6144]{1,0:T(8,128)(2,1)} fusion(bf16[1024,2048]{1,0:T(8,128)(2,1)S(1)} %convolution_convert_fusion, bf16[1024,2048]{1,0:T(8,128)(2,1)S(1)} %convolution_convert_fusion.1, bf16[1024,2048]{1,0:T(8,128)(2,1)S(1)} %convolution_convert_fusion.2), kind=kLoop, calls=%fused_computation | loop fusion | flops 37748736 | bytes 25165824 | tf_op jit(solution)/shard_map/concatenate | solution.py:72
  233.0 0.2 all-gather.2.cloned.1.call-start
  233.3 0.4 copy-done.9
  233.7 0.2 fusion.39
  234.0 122.2 %reduce-scatter.2.cloned.1.call-done = bf16[64,6144]{1,0:T(8,128)(2,1)} async-done(((bf16[1024,6144]{1,0:T(8,128)(2,1)}), bf16[64,6144]{1,0:T(8,128)(2,1)}) %reduce-scatter.2.cloned.1.call-update) | async-done | bytes 786448 | tf_op jit(solution)/shard_map/reduce_scatter | solution.py:71
  356.2 1.2 convert_element_type.43
  357.4 0.4 multiply_convert_fusion.5
  357.8 0.9 pad_maximum_fusion.1
  358.8 91.2 %all-gather.2.cloned.1.call-done = bf16[1024,6144]{1,0:T(8,128)(2,1)} async-done(((bf16[64,6144]{1,0:T(8,128)(2,1)}), bf16[1024,6144]{1,0:T(8,128)(2,1)}) %all-gather.2.cloned.1.call-update) | async-done | bytes 12582928 | tf_op jit(solution)/shard_map/all_gather | solution.py:85
  449.9 4.4 fusion.4
  454.3 4.4 fusion.34
  458.7 3.9 copy.90
  462.6 8.3 %reduce.4 = bf16[1024,448]{1,0:T(8,128)(2,1)S(1)} reduce(bf16[1024,1,448]{2,1,0:T(2,128)(2,1)} %bitcast.98, bf16[]{:T(256)} %broadcast.46), dimensions={1}, to_apply=%bitcast.74.reduce_sub_computation | reduce | bytes 1835010
  470.9 2.1 reshape.72
  473.0 3.9 all-to-all-start.4
  476.9 5.8 fusion.16
  482.7 10.2 %all-to-all-done.4 = bf16[16,2,14336]{2,1,0:T(2,128)(2,1)S(1)} async-done(((bf16[16,2,14336]{2,1,0:T(2,128)(2,1)}), bf16[16,2,14336]{2,1,0:T(2,128)(2,1)S(1)}, u32[]{:S(2)}, u32[]{:S(2)}) %all-to-all-start.4) | async-done | bytes 917536 | tf_op jit(solution)/shard_map/all_to_all | solution.py:100
  492.9 3.7 reshape.73
  496.6 1.9 copy.102
  498.5 1.7 copy.98
  500.2 11.1 %reshape.66 = bf16[1,64,7168]{1,0,2:T(2,128)(2,1)} reshape(bf16[1,64,16,448]{1,3,2,0:T(8,128)(2,1)} %copy.98) | data formatting | bytes 1835008 | tf_op jit(solution)/shard_map/all_to_all | solution.py:100
  511.3 41.0 %reduce.5 = bf16[7168,64]{1,0:T(8,128)(2,1)} reduce(bf16[7168,1,64]{2,1,0:T(2,128)(2,1)} %bitcast.93, bf16[]{:T(256)} %broadcast.46), dimensions={1}, to_apply=%bitcast.76.reduce_sub_computation | reduce | bytes 1835010
  552.3 4.3 reshape.74
  556.6 4.4 all-to-all-start.5
  561.0 5.9 fusion.19
  566.9 5.5 fusion.22
  572.5 2.9 all-to-all-done.5
  575.4 4.1 reshape.75
  579.5 7.2 %copy.93 = bf16[1,64,7168]{2,1,0:T(8,128)(2,1)S(1)} copy(bf16[1,64,7168]{1,0,2:T(2,128)(2,1)} %bitcast.97) | data formatting | bytes 1835008 | tf_op jit(solution)/shard_map/all_to_all | solution.py:99
  586.7 0.1 copy.103
  587.1 1.0 convolution_convert_fusion.5
  (35 shorter events, 1.1 us)
Async XLA Ops:
  7.2 207.4 %copy-start = (bf16[1,448,2048]{2,1,0:T(8,128)(2,1)S(1)}, bf16[1,448,2048]{2,1,0:T(8,128)(2,1)}, u32[]{:S(2)}) copy-start(bf16[1,448,2048]{2,1,0:T(8,128)(2,1)} %param.12) | copy-start | bytes 5505028
  7.2 11.8 %copy-start.5 = (bf16[128,896]{1,0:T(8,128)(2,1)S(1)}, bf16[128,896]{1,0:T(8,128)(2,1)}, u32[]{:S(2)}) copy-start(bf16[128,896]{1,0:T(8,128)(2,1)} %param.7) | copy-start | bytes 688132
  12.6 20.8 %all-to-all-start.2 = ((bf16[8,64,896]{2,1,0:T(8,128)(2,1)}), bf16[8,64,896]{2,1,0:T(8,128)(2,1)S(1)}, u32[]{:S(2)}, u32[]{:S(2)}) async-start(bf16[8,64,896]{2,1,0:T(8,128)(2,1)} %bitcast.12), calls=%async_computation.2 | async-start | bytes 1835008 | tf_op jit(solution)/shard_map/all_to_all | solution.py:53
  33.4 0.9 copy-start.1
  34.3 63.0 %all-to-all-start = ((bf16[8,64,896]{2,1,0:T(8,128)(2,1)}), bf16[8,64,896]{2,1,0:T(8,128)(2,1)S(1)}, u32[]{:S(2)}, u32[]{:S(2)}) async-start(bf16[8,64,896]{2,1,0:T(8,128)(2,1)} %bitcast.5), calls=%async_computation | async-start | bytes 1835008 | tf_op jit(solution)/shard_map/all_to_all | solution.py:46
  97.3 66.6 %all-to-all-start.3 = ((bf16[16,2,14336]{2,1,0:T(2,128)(2,1)}), bf16[16,2,14336]{2,1,0:T(2,128)(2,1)}, u32[]{:S(2)}, u32[]{:S(2)}) async-start(bf16[16,2,14336]{2,1,0:T(2,128)(2,1)} %reshape.68), calls=%async_computation.3 | async-start | bytes 1835008 | tf_op jit(solution)/shard_map/all_to_all | solution.py:52
  163.9 29.7 %all-to-all-start.1 = ((bf16[16,2,14336]{2,1,0:T(2,128)(2,1)}), bf16[16,2,14336]{2,1,0:T(2,128)(2,1)}, u32[]{:S(2)}, u32[]{:S(2)}) async-start(bf16[16,2,14336]{2,1,0:T(2,128)(2,1)} %reshape.70), calls=%async_computation.1 | async-start | bytes 1835008 | tf_op jit(solution)/shard_map/all_to_all | solution.py:45
  171.2 185.0 %reduce-scatter.2.cloned.1.call-start = ((), (), s32[]{:S(2)}) async-start(), calls=%async_computation.7 | async-start | bytes 13369344 | tf_op jit(solution)/shard_map/reduce_scatter | solution.py:71
  214.6 2.4 copy-start.4
  214.6 2.4 copy-start.7
  217.0 2.4 copy-start.2
  217.0 2.4 copy-start.6
  233.0 0.7 copy-start.9
  233.0 216.9 %all-gather.2.cloned.1.call-start = ((), (), s32[]{:S(2)}) async-start(), calls=%async_computation.8 | async-start | bytes 13369344 | tf_op jit(solution)/shard_map/all_gather | solution.py:85
  449.9 4.4 copy-start.8
  473.0 19.9 %all-to-all-start.4 = ((bf16[16,2,14336]{2,1,0:T(2,128)(2,1)}), bf16[16,2,14336]{2,1,0:T(2,128)(2,1)S(1)}, u32[]{:S(2)}, u32[]{:S(2)}) async-start(bf16[16,2,14336]{2,1,0:T(2,128)(2,1)} %reshape.72), calls=%async_computation.5 | async-start | bytes 1835008 | tf_op jit(solution)/shard_map/all_to_all | solution.py:100
  556.6 18.8 %all-to-all-start.5 = ((bf16[8,2,28672]{2,1,0:T(2,128)(2,1)}), bf16[8,2,28672]{2,1,0:T(2,128)(2,1)S(1)}, u32[]{:S(2)}, u32[]{:S(2)}) async-start(bf16[8,2,28672]{2,1,0:T(2,128)(2,1)} %reshape.74), calls=%async_computation.6 | async-start | bytes 1835008 | tf_op jit(solution)/shard_map/all_to_all | solution.py:99
  561.0 5.9 copy-start.3
Sparse Core Ops, SparseCore 0:
  233.1 123.0 reduce-scatter.1
  359.5 90.3 all-gather.1
where the time goes:
time: 606 us; the launch traced here: 595 us
  waiting for transfers between devices  240 us (40%)
  other arithmetic  147 us (24%)
  local copies, waits for them, and re-layouts  122 us (20%)
  matrix products  37.9 us (6%)
  starting transfers between devices  34.6 us (6%)
  between operations  14.8 us (2%)
    unnamed x4, other arithmetic  131 us
    reduce_scatter x1, waiting for transfers between devices, body(): lax.psum_scatter(jnp.concatenate([gate, upper, back], axis=1).astype(jnp....  122 us
    all_gather x1, waiting for transfers between devices, body(): piece = lax.all_gather(local, 'dp', axis=0, tiled=True)  91.2 us
    unnamed x32, local copies, waits for them, and re-layouts  47.4 us
    all_to_all x2, local copies, waits for them, and re-layouts, body(): lax.all_to_all(send_g, 'expert', split_axis=0, concat_axis=2, tiled=True)  13.7 us
    all_to_all x1, waiting for transfers between devices, body(): lax.all_to_all(send_g, 'expert', split_axis=0, concat_axis=2, tiled=True)  13.1 us
    all_to_all x2, local copies, waits for them, and re-layouts, body(): lax.all_to_all(dx_rows.reshape(1, slots, shard_width), 'dp', split_axis=1...  12.8 us
    all_to_all x2, local copies, waits for them, and re-layouts, body(): lax.all_to_all(send_x, 'expert', split_axis=0, concat_axis=2, tiled=True)  12.8 us
  transfers between devices with their start and end apart: 8, of which 5 were waited for; matrix products, arithmetic and copies ran while one was open for 26% of the time, Pallas kernels for 0%

commit v1 on v0

--- a/solution.py
+++ b/solution.py
@@ -82,7 +82,12 @@
     d_gate = back * upper * sigmoid_gate * (1.0 + gate * (1.0 - sigmoid_gate))
     d_up = back * gate * sigmoid_gate
     local = jnp.concatenate([scaled, d_gate, d_up], axis=1).astype(jnp.bfloat16)
-    piece = lax.all_gather(local, "dp", axis=0, tiled=True)
+    piece = jnp.concatenate(
+        lax.all_to_all(
+            jnp.stack([local] * lax.psum(1, "dp")), axis_name="dp", split_axis=0, concat_axis=0
+        ),
+        axis=0,
+    )
     x_block = feature_rows
     g_block = grad_rows
     scaled = piece[:, :hidden]

time: 606 us -> 666 us (1.099)
  blocking collectives: 0 us -> 146 us
  waiting for transfers between devices: 240 us -> 148 us
  local copies, waits for them, and re-layouts: 122 us -> 131 us
    all_to_all x0 -> x1, blocking collectives: none -> 146 us  [body(): lax.all_to_all(jnp.stack([local] * lax.psum(1, 'dp')), axis_name='dp', sp...]
    all_gather x1 -> x0, waiting for transfers between devices: 91.2 us -> none  [body(): piece = lax.all_gather(local, 'dp', axis=0, tiled=True)]
    unnamed x32 -> x34, local copies, waits for them, and re-layouts: 47.4 us -> 50.4 us
  transfers between devices with their start and end apart: 8 -> 7, of which waited for: 5 -> 4; matrix products, arithmetic and copies ran while one was open for 26% -> 24% of each run, Pallas kernels for 0% -> 0%
where the time goes in v1:
time: 666 us; the launch traced here: 655 us
  waiting for transfers between devices  148 us (22%)
  other arithmetic  146 us (22%)
  blocking collectives  146 us (22%)
  local copies, waits for them, and re-layouts  131 us (20%)
  starting transfers between devices  35.6 us (5%)
  matrix products  33.3 us (5%)
  between operations  14.8 us (2%)
    all_to_all x1, blocking collectives, body(): lax.all_to_all(jnp.stack([local] * lax.psum(1, 'dp')), axis_name='dp', sp...  146 us
    unnamed x4, other arithmetic  131 us
    reduce_scatter x1, waiting for transfers between devices, body(): lax.psum_scatter(jnp.concatenate([gate, upper, back], axis=1).astype(jnp....  122 us
    unnamed x34, local copies, waits for them, and re-layouts  50.4 us
    all_to_all x2, local copies, waits for them, and re-layouts, body(): lax.all_to_all(send_g, 'expert', split_axis=0, concat_axis=2, tiled=True)  13.7 us
  transfers between devices with their start and end apart: 7, of which 4 were waited for; matrix products, arithmetic and copies ran while one was open for 24% of the time, Pallas kernels for 0%

profile of v1, /device:TPU:1, one launch (start us, length us, event | category | flops | bytes accessed | tf_op | source)
XLA Modules:
  0.0 654.7 jit_solution(2940743966294731631)
XLA Ops:
  7.2 0.9 copy.79
  8.4 0.6 reduce-window.6
  9.0 0.2 slice_reduce_fusion
  9.6 0.7 compare_select_fusion
  10.3 2.3 convolution_convert_fusion.3
  12.6 6.4 all-to-all-start.2
  19.0 1.3 convolution_convert_fusion.4
  20.3 13.1 %all-to-all-done.2 = bf16[8,64,896]{2,1,0:T(8,128)(2,1)S(1)} async-done(((bf16[8,64,896]{2,1,0:T(8,128)(2,1)}), bf16[8,64,896]{2,1,0:T(8,128)(2,1)S(1)}, u32[]{:S(2)}, u32[]{:S(2)}) %all-to-all-start.2) | async-done | bytes 917536 | tf_op jit(solution)/shard_map/all_to_all | solution.py:53
  33.4 0.9 copy-done.2
  34.3 3.6 all-to-all-start
  37.9 2.6 copy.97
  40.4 11.1 %reshape.79 = bf16[1,64,7168]{1,0,2:T(2,128)(2,1)} reshape(bf16[1,64,8,896]{1,3,2,0:T(8,128)(2,1)} %copy.97) | data formatting | bytes 1835008 | tf_op jit(solution)/shard_map/all_to_all | solution.py:53
  51.6 0.5 broadcast.47
  52.1 41.0 %reduce.2 = bf16[7168,64]{1,0:T(8,128)(2,1)} reduce(bf16[7168,1,64]{2,1,0:T(2,128)(2,1)} %bitcast.93, bf16[]{:T(256)} %broadcast.47), dimensions={1}, to_apply=%bitcast.71.reduce_sub_computation | reduce | bytes 1835010
  93.1 4.3 reshape.82
  97.3 8.5 %all-to-all-start.3 = ((bf16[16,2,14336]{2,1,0:T(2,128)(2,1)}), bf16[16,2,14336]{2,1,0:T(2,128)(2,1)}, u32[]{:S(2)}, u32[]{:S(2)}) async-start(bf16[16,2,14336]{2,1,0:T(2,128)(2,1)} %reshape.82), calls=%async_computation.3 | async-start | bytes 1835008 | tf_op jit(solution)/shard_map/all_to_all | solution.py:52
  105.9 1.7 copy.96
  107.5 11.1 %reshape.78 = bf16[1,64,7168]{1,0,2:T(2,128)(2,1)} reshape(bf16[1,64,8,896]{1,3,2,0:T(8,128)(2,1)} %copy.96) | data formatting | bytes 1835008 | tf_op jit(solution)/shard_map/all_to_all | solution.py:46
  118.7 41.0 %reduce.3 = bf16[7168,64]{1,0:T(8,128)(2,1)} reduce(bf16[7168,1,64]{2,1,0:T(2,128)(2,1)} %bitcast.95, bf16[]{:T(256)} %broadcast.47), dimensions={1}, to_apply=%bitcast.73.reduce_sub_computation | reduce | bytes 1835010
  159.7 4.3 reshape.84
  163.9 7.2 %all-to-all-start.1 = ((bf16[16,2,14336]{2,1,0:T(2,128)(2,1)}), bf16[16,2,14336]{2,1,0:T(2,128)(2,1)}, u32[]{:S(2)}, u32[]{:S(2)}) async-start(bf16[16,2,14336]{2,1,0:T(2,128)(2,1)} %reshape.84), calls=%async_computation.1 | async-start | bytes 1835008 | tf_op jit(solution)/shard_map/all_to_all | solution.py:45
  171.2 0.4 reduce-scatter.2.cloned.1.call-start
  171.6 9.9 %reshape.83 = bf16[7168,1,64]{2,1,0:T(2,128)(2,1)} reshape(bf16[16,2,14336]{2,1,0:T(2,128)(2,1)} %all-to-all-done.3) | data formatting | bytes 1835008
  181.5 8.1 %copy.88 = bf16[1,64,7168]{2,1,0:T(8,128)(2,1)} copy(bf16[1,64,7168]{1,0,2:T(2,128)(2,1)} %bitcast.96) | data formatting | bytes 1835008 | tf_op jit(solution)/shard_map/all_to_all | solution.py:52
  189.7 2.3 all_to_all.87
  192.0 1.6 copy.89
  193.6 9.9 %reshape.85 = bf16[7168,1,64]{2,1,0:T(2,128)(2,1)} reshape(bf16[16,2,14336]{2,1,0:T(2,128)(2,1)} %all-to-all-done.1) | data formatting | bytes 1835008
  203.5 8.1 %copy.84 = bf16[1,64,7168]{2,1,0:T(8,128)(2,1)} copy(bf16[1,64,7168]{1,0,2:T(2,128)(2,1)} %bitcast.97) | data formatting | bytes 1835008 | tf_op jit(solution)/shard_map/all_to_all | solution.py:45
  211.7 2.3 all_to_all.80
  214.0 0.6 copy.85
  214.6 2.3 convolution_convert_fusion.1
  217.0 2.3 convolution_convert_fusion.2
  219.4 2.3 convolution_convert_fusion
  221.7 11.3 %pad_maximum_fusion = bf16[1024,6144]{1,0:T(8,128)(2,1)} fusion(bf16[1024,2048]{1,0:T(8,128)(2,1)S(1)} %convolution_convert_fusion, bf16[1024,2048]{1,0:T(8,128)(2,1)S(1)} %convolution_convert_fusion.1, bf16[1024,2048]{1,0:T(8,128)(2,1)S(1)} %convolution_convert_fusion.2), kind=kLoop, calls=%fused_computation | loop fusion | flops 37748736 | bytes 25165824 | tf_op jit(solution)/shard_map/concatenate | solution.py:72
  233.0 0.6 copy-done.10
  233.7 0.2 fusion.39
  234.0 122.2 %reduce-scatter.2.cloned.1.call-done = bf16[64,6144]{1,0:T(8,128)(2,1)} async-done(((bf16[1024,6144]{1,0:T(8,128)(2,1)}), bf16[64,6144]{1,0:T(8,128)(2,1)}) %reduce-scatter.2.cloned.1.call-update) | async-done | bytes 786448 | tf_op jit(solution)/shard_map/reduce_scatter | solution.py:71
  356.2 1.2 convert_element_type.45
  357.4 0.4 multiply_convert_fusion.5
  357.9 6.1 stack.2
  364.0 145.9 %all_to_all.104 = bf16[16,64,6144]{2,1,0:T(8,128)(2,1)S(1)} all-to-all(bf16[16,64,6144]{2,1,0:T(8,128)(2,1)} %stack.2), channel_id=1, replica_groups=mesh['expert'=8,'dp'=16] {'dp'}, dimensions={0} | all-to-all | bytes 25165824 | tf_op jit(solution)/shard_map/all_to_all | solution.py:86
  509.9 2.1 fusion.4
  512.0 2.7 copy-done.1
  514.7 2.1 fusion.34
  516.8 3.9 copy.90
  520.7 8.3 %reduce.4 = bf16[1024,448]{1,0:T(8,128)(2,1)S(1)} reduce(bf16[1024,1,448]{2,1,0:T(2,128)(2,1)} %bitcast.104, bf16[]{:T(256)} %broadcast.47), dimensions={1}, to_apply=%bitcast.75.reduce_sub_computation | reduce | bytes 1835010
  529.0 2.1 reshape.86
  531.1 4.8 all-to-all-start.5
  535.9 5.8 fusion.16
  541.7 10.1 %all-to-all-done.5 = bf16[16,2,14336]{2,1,0:T(2,128)(2,1)S(1)} async-done(((bf16[16,2,14336]{2,1,0:T(2,128)(2,1)}), bf16[16,2,14336]{2,1,0:T(2,128)(2,1)S(1)}, u32[]{:S(2)}, u32[]{:S(2)}) %all-to-all-start.5) | async-done | bytes 917536 | tf_op jit(solution)/shard_map/all_to_all | solution.py:105
  551.9 3.7 reshape.87
  555.6 1.9 copy.102
  557.5 1.7 copy.98
  559.1 11.1 %reshape.80 = bf16[1,64,7168]{1,0,2:T(2,128)(2,1)} reshape(bf16[1,64,16,448]{1,3,2,0:T(8,128)(2,1)} %copy.98) | data formatting | bytes 1835008 | tf_op jit(solution)/shard_map/all_to_all | solution.py:105
  570.3 41.0 %reduce.5 = bf16[7168,64]{1,0:T(8,128)(2,1)} reduce(bf16[7168,1,64]{2,1,0:T(2,128)(2,1)} %bitcast.94, bf16[]{:T(256)} %broadcast.47), dimensions={1}, to_apply=%bitcast.77.reduce_sub_computation | reduce | bytes 1835010
  611.3 4.3 reshape.88
  615.6 4.7 all-to-all-start.6
  620.3 5.9 fusion.19
  626.2 5.5 fusion.22
  631.7 2.9 all-to-all-done.6
  634.7 4.1 reshape.89
  638.8 7.2 %copy.93 = bf16[1,64,7168]{2,1,0:T(8,128)(2,1)S(1)} copy(bf16[1,64,7168]{1,0,2:T(2,128)(2,1)} %bitcast.98) | data formatting | bytes 1835008 | tf_op jit(solution)/shard_map/all_to_all | solution.py:104
  646.0 0.1 copy.103
  646.4 1.0 convolution_convert_fusion.5
  (36 shorter events, 1.1 us)
Async XLA Ops:
  7.2 207.4 %copy-start = (bf16[1,448,2048]{2,1,0:T(8,128)(2,1)S(1)}, bf16[1,448,2048]{2,1,0:T(8,128)(2,1)}, u32[]{:S(2)}) copy-start(bf16[1,448,2048]{2,1,0:T(8,128)(2,1)} %param.12) | copy-start | bytes 5505028
  7.2 11.8 %copy-start.6 = (bf16[128,896]{1,0:T(8,128)(2,1)S(1)}, bf16[128,896]{1,0:T(8,128)(2,1)}, u32[]{:S(2)}) copy-start(bf16[128,896]{1,0:T(8,128)(2,1)} %param.7) | copy-start | bytes 688132
  12.6 20.8 %all-to-all-start.2 = ((bf16[8,64,896]{2,1,0:T(8,128)(2,1)}), bf16[8,64,896]{2,1,0:T(8,128)(2,1)S(1)}, u32[]{:S(2)}, u32[]{:S(2)}) async-start(bf16[8,64,896]{2,1,0:T(8,128)(2,1)} %bitcast.12), calls=%async_computation.2 | async-start | bytes 1835008 | tf_op jit(solution)/shard_map/all_to_all | solution.py:53
  33.4 0.9 copy-start.2
  34.3 63.0 %all-to-all-start = ((bf16[8,64,896]{2,1,0:T(8,128)(2,1)}), bf16[8,64,896]{2,1,0:T(8,128)(2,1)S(1)}, u32[]{:S(2)}, u32[]{:S(2)}) async-start(bf16[8,64,896]{2,1,0:T(8,128)(2,1)} %bitcast.5), calls=%async_computation | async-start | bytes 1835008 | tf_op jit(solution)/shard_map/all_to_all | solution.py:46
  97.3 66.6 %all-to-all-start.3 = ((bf16[16,2,14336]{2,1,0:T(2,128)(2,1)}), bf16[16,2,14336]{2,1,0:T(2,128)(2,1)}, u32[]{:S(2)}, u32[]{:S(2)}) async-start(bf16[16,2,14336]{2,1,0:T(2,128)(2,1)} %reshape.82), calls=%async_computation.3 | async-start | bytes 1835008 | tf_op jit(solution)/shard_map/all_to_all | solution.py:52
  163.9 29.7 %all-to-all-start.1 = ((bf16[16,2,14336]{2,1,0:T(2,128)(2,1)}), bf16[16,2,14336]{2,1,0:T(2,128)(2,1)}, u32[]{:S(2)}, u32[]{:S(2)}) async-start(bf16[16,2,14336]{2,1,0:T(2,128)(2,1)} %reshape.84), calls=%async_computation.1 | async-start | bytes 1835008 | tf_op jit(solution)/shard_map/all_to_all | solution.py:45
  171.2 185.0 %reduce-scatter.2.cloned.1.call-start = ((), (), s32[]{:S(2)}) async-start(), calls=%async_computation.8 | async-start | bytes 13369344 | tf_op jit(solution)/shard_map/reduce_scatter | solution.py:71
  214.6 2.4 copy-start.5
  214.6 2.4 copy-start.8
  217.0 2.4 copy-start.3
  217.0 2.4 copy-start.7
  233.0 0.7 copy-start.10
  509.9 4.8 copy-start.1
  509.9 4.8 copy-start.9
  531.1 20.8 %all-to-all-start.5 = ((bf16[16,2,14336]{2,1,0:T(2,128)(2,1)}), bf16[16,2,14336]{2,1,0:T(2,128)(2,1)S(1)}, u32[]{:S(2)}, u32[]{:S(2)}) async-start(bf16[16,2,14336]{2,1,0:T(2,128)(2,1)} %reshape.86), calls=%async_computation.6 | async-start | bytes 1835008 | tf_op jit(solution)/shard_map/all_to_all | solution.py:105
  615.6 19.1 %all-to-all-start.6 = ((bf16[8,2,28672]{2,1,0:T(2,128)(2,1)}), bf16[8,2,28672]{2,1,0:T(2,128)(2,1)S(1)}, u32[]{:S(2)}, u32[]{:S(2)}) async-start(bf16[8,2,28672]{2,1,0:T(2,128)(2,1)} %reshape.88), calls=%async_computation.7 | async-start | bytes 1835008 | tf_op jit(solution)/shard_map/all_to_all | solution.py:104
  620.3 5.9 copy-start.4
Sparse Core Ops, SparseCore 0:
  233.1 123.0 reduce-scatter.1
